TPU v7x, 32 devices: a whole 2x2x4 slice. The times are simulated.
32 devices in a mesh: fsdp: 32 (over z, y, x, core).
Axes of the slice: x: 2, y: 2, z: 4, core: 2. Of those that a mesh axis runs over, the one named last changes fastest.
Arguments:
- tokens: bfloat16 [65536, 768], P('fsdp'), may hold values from -6 to 6
- cotangent: bfloat16 [65536, 768], P('fsdp'), may hold values from -6 to 6
- segments: int32 [65536], P('fsdp'), may hold values from 0 to 1, as said below
- positions: int32 [65536], P('fsdp'), may hold values from 0 to 1999, as said below
- qkv_weight: float32 [768, 2304], P('fsdp'), may hold values from -0.21875 to 0.21875
- qkv_first: float32 [768, 2304], P('fsdp'), may hold values from -160 to 160
- qkv_second: float32 [768, 2304], P('fsdp'), may hold values from 1310 to 5461
- out_weight: float32 [768, 768], P('fsdp'), may hold values from -0.625 to 0.625
- out_first: float32 [768, 768], P('fsdp'), may hold values from -160 to 160
- out_second: float32 [768, 768], P('fsdp'), may hold values from 1310 to 5461
- in_weight: float32 [768, 2304], P('fsdp'), may hold values from -0.21875 to 0.21875
- in_first: float32 [768, 2304], P('fsdp'), may hold values from -160 to 160
- in_second: float32 [768, 2304], P('fsdp'), may hold values from 1310 to 5461
- down_weight: float32 [1152, 768], P('fsdp'), may hold values from -0.375 to 0.375
- down_first: float32 [1152, 768], P('fsdp'), may hold values from -160 to 160
- down_second: float32 [1152, 768], P('fsdp'), may hold values from 1310 to 5461
- norm_gains: float32 [2, 768], P(None, 'fsdp'), may hold values from 0.5 to 1.5
- gains_first: float32 [2, 768], P(None, 'fsdp'), may hold values from -160 to 160
- gains_second: float32 [2, 768], P(None, 'fsdp'), may hold values from 1310 to 5461
Outputs:
- activations: bfloat16 [65536, 768], P('fsdp')
- input_grad: float32 [65536, 768], P('fsdp')
- qkv_grad: float32 [768, 2304], P('fsdp')
- qkv_new: float32 [768, 2304], P('fsdp')
- qkv_first_new: float32 [768, 2304], P('fsdp')
- qkv_second_new: float32 [768, 2304], P('fsdp')
- out_grad: float32 [768, 768], P('fsdp')
- out_new: float32 [768, 768], P('fsdp')
- out_first_new: float32 [768, 768], P('fsdp')
- out_second_new: float32 [768, 768], P('fsdp')
- in_grad: float32 [768, 2304], P('fsdp')
- in_new: float32 [768, 2304], P('fsdp')
- in_first_new: float32 [768, 2304], P('fsdp')
- in_second_new: float32 [768, 2304], P('fsdp')
- down_grad: float32 [1152, 768], P('fsdp')
- down_new: float32 [1152, 768], P('fsdp')
- down_first_new: float32 [1152, 768], P('fsdp')
- down_second_new: float32 [1152, 768], P('fsdp')
- gains_grad: float32 [2, 768], P(None, 'fsdp')
- gains_delta: float32 [2, 768], P(None, 'fsdp')
- gains_first_new: float32 [2, 768], P(None, 'fsdp')
- gains_second_new: float32 [2, 768], P(None, 'fsdp')
Inputs may be any that keep to these rules, and one draw needn't show every extreme that they name: `segments`: documents lie end to end over all 65536 tokens; the segment number is 0 on the first document and changes between 0 and 1 from each document to the next. Each document is 200 to 2000 tokens long, the last cut at the end, and both lengths occur. A document may run across packed sequences. `positions`: place of each token in its document counted from 0; it grows by one from token to token inside a document and starts again at 0 where the segment number changes.
All inputs are finite; a program needn't handle non-finite values.
Results may differ from a plain program's by a relative error of at most 0.019.
Values may be sent and summed in bfloat16 or wider, within the bound.
A program may use at most 256 MiB of HBM per device.

v0:
```python
import jax
import jax.numpy as jnp
from jax import lax
from jax.sharding import PartitionSpec as P

D = 768
HEADS = 12
HEAD = 64
FF = 1152
SEQ = 512
BLK = 128
STEP = 10
NORM_EPS = 1e-05
BETA_ONE = 0.9
BETA_TWO = 0.98
ADAM_EPS = 1e-06
LEARN_RATE = 0.1
WEIGHT_DECAY = 0.01
ROPE_BASE = 10000.0
MASKED = -1e30


def layer_norm(values, norm_gain):
    center = values - jnp.mean(values, axis=-1, keepdims=True)
    spread = jnp.mean(center * center, axis=-1, keepdims=True)
    return center * lax.rsqrt(spread + NORM_EPS) * norm_gain


def rotate(values, cosine, sine):
    half_dim = values.shape[-1] // 2
    turned = jnp.concatenate([-values[..., half_dim:], values[..., :half_dim]], axis=-1)
    return values * cosine + turned * sine


def rope_tables(places):
    half_dim = HEAD // 2
    frequency = ROPE_BASE ** (-(jnp.arange(half_dim).astype(jnp.float32) * 2.0 / HEAD))
    angles = places.astype(jnp.float32)[:, None] * frequency[None, :]
    angles = jnp.concatenate([angles, angles], axis=-1)
    return (jnp.cos(angles)[:, None, :], jnp.sin(angles)[:, None, :])


def widen(blocked):
    before = jnp.roll(blocked, 1, axis=0)
    after = jnp.roll(blocked, -1, axis=0)
    return jnp.concatenate([before, blocked, after], axis=1)


def fold_wide(wide):
    block_width = wide.shape[1] // 3
    middle = wide[:, block_width : 2 * block_width]
    return (
        middle
        + jnp.roll(wide[:, :block_width], -1, axis=0)
        + jnp.roll(wide[:, 2 * block_width :], 1, axis=0)
    )


def window_mask(seq_segs, block_width):
    row_count = seq_segs.shape[0]
    block_count = row_count // block_width
    starts = jnp.arange(block_count)[:, None, None] * block_width
    query_at = starts + jnp.arange(block_width)[None, :, None]
    key_at = starts - block_width + jnp.arange(3 * block_width)[None, None, :]
    seg_blocks = seq_segs.reshape(block_count, block_width)
    seg_wide = widen(seg_blocks)
    in_window = jnp.abs(query_at - key_at) <= block_width // 2
    inside = (key_at >= 0) & (key_at < row_count)
    same_doc = seg_blocks[:, :, None] == seg_wide[:, None, :]
    return in_window & inside & same_doc


def block_scores(query_heads, key_heads, seq_segs):
    block_count = query_heads.shape[0] // BLK
    query_blocks = query_heads.reshape(block_count, BLK, HEADS, HEAD)
    key_wide = widen(key_heads.reshape(block_count, BLK, HEADS, HEAD))
    scores = jnp.einsum(
        "bqhe,bkhe->bhqk", query_blocks, key_wide, preferred_element_type=jnp.float32
    ) * HEAD ** (-0.5)
    allowed = window_mask(seq_segs, BLK)[:, None]
    return (jnp.where(allowed, scores, MASKED), query_blocks, key_wide)


def attend(seq_items):
    query_heads, key_heads, value_heads, seq_segs = seq_items
    scores, query_blocks, key_wide = block_scores(query_heads, key_heads, seq_segs)
    row_top = jnp.max(scores, axis=-1, keepdims=True)
    exp_scores = jnp.exp(scores - row_top)
    row_total = jnp.sum(exp_scores, axis=-1, keepdims=True)
    prob_low = (exp_scores / row_total).astype(jnp.bfloat16)
    value_wide = widen(value_heads.reshape(query_blocks.shape))
    attended = jnp.einsum(
        "bhqk,bkhe->bqhe", prob_low, value_wide, preferred_element_type=jnp.float32
    )
    return (attended.reshape(value_heads.shape).astype(jnp.bfloat16), row_top + jnp.log(row_total))


def attend_back(seq_items):
    query_heads, key_heads, value_heads, grad_heads, log_total, seq_segs = seq_items
    scores, query_blocks, key_wide = block_scores(query_heads, key_heads, seq_segs)
    value_wide = widen(value_heads.reshape(query_blocks.shape))
    grad_blocks = grad_heads.reshape(query_blocks.shape)
    attn_prob = jnp.exp(scores - log_total)
    prob_low = attn_prob.astype(jnp.bfloat16)
    grad_value_wide = jnp.einsum(
        "bhqk,bqhe->bkhe", prob_low, grad_blocks, preferred_element_type=jnp.float32
    )
    grad_prob = jnp.einsum(
        "bqhe,bkhe->bhqk", grad_blocks, value_wide, preferred_element_type=jnp.float32
    )
    inner = jnp.sum(attn_prob * grad_prob, axis=-1, keepdims=True)
    grad_scores = (attn_prob * (grad_prob - inner)).astype(jnp.bfloat16)
    scale_factor = HEAD ** (-0.5)
    grad_query = (
        jnp.einsum("bhqk,bkhe->bqhe", grad_scores, key_wide, preferred_element_type=jnp.float32)
        * scale_factor
    )
    grad_key_wide = (
        jnp.einsum("bhqk,bqhe->bkhe", grad_scores, query_blocks, preferred_element_type=jnp.float32)
        * scale_factor
    )
    head_shape = query_heads.shape
    return (
        grad_query.reshape(head_shape),
        fold_wide(grad_key_wide).reshape(head_shape),
        fold_wide(grad_value_wide).reshape(head_shape),
    )


def split_seqs(array, seq_count):
    return array.reshape((seq_count, SEQ) + array.shape[1:])


def adam_step(master, weight_grad, moment_one, moment_two):
    first_new = BETA_ONE * moment_one + (1.0 - BETA_ONE) * weight_grad
    second_new = BETA_TWO * moment_two + (1.0 - BETA_TWO) * weight_grad * weight_grad
    first_hat = first_new / (1.0 - BETA_ONE**STEP)
    second_hat = second_new / (1.0 - BETA_TWO**STEP)
    master_new = master - LEARN_RATE * (
        first_hat / (jnp.sqrt(second_hat) + ADAM_EPS) + WEIGHT_DECAY * master
    )
    return (weight_grad, master_new, first_new, second_new)


def geglu(gate_up):
    return jax.nn.gelu(gate_up[:, :FF], approximate=False) * gate_up[:, FF:]


def shards(
    tokens,
    cotangent,
    segments,
    positions,
    qkv_weight,
    qkv_first,
    qkv_second,
    out_weight,
    out_first,
    out_second,
    in_weight,
    in_first,
    in_second,
    down_weight,
    down_first,
    down_second,
    norm_gains,
    gains_first,
    gains_second,
):
    masters = (qkv_weight, out_weight, in_weight, down_weight, norm_gains)
    rounded = tuple((master.astype(jnp.bfloat16) for master in masters))
    gathered = (
        lax.all_gather(rounded[0], "fsdp", axis=0, tiled=True),
        lax.all_gather(rounded[1], "fsdp", axis=0, tiled=True),
        lax.all_gather(rounded[2], "fsdp", axis=0, tiled=True),
        lax.all_gather(rounded[3], "fsdp", axis=0, tiled=True),
        lax.all_gather(rounded[4], "fsdp", axis=1, tiled=True),
    )
    qkv_low, out_low, in_low, down_low, gains_low = gathered
    gains_full = gains_low.astype(jnp.float32)
    row_count = tokens.shape[0]
    seq_count = row_count // SEQ
    hidden_in = tokens.astype(jnp.float32)
    normed, norm_back_one = jax.vjp(layer_norm, hidden_in, gains_full[0])
    normed_low = normed.astype(jnp.bfloat16)
    qkv_mixed = jnp.dot(normed_low, qkv_low, preferred_element_type=jnp.float32)
    cosine, sine = rope_tables(positions)
    query_heads = rotate(qkv_mixed[:, :D].reshape(row_count, HEADS, HEAD), cosine, sine).astype(
        jnp.bfloat16
    )
    key_heads = rotate(
        qkv_mixed[:, D : 2 * D].reshape(row_count, HEADS, HEAD), cosine, sine
    ).astype(jnp.bfloat16)
    value_heads = qkv_mixed[:, 2 * D :].reshape(row_count, HEADS, HEAD).astype(jnp.bfloat16)
    seq_queries = split_seqs(query_heads, seq_count)
    seq_keys = split_seqs(key_heads, seq_count)
    seq_values = split_seqs(value_heads, seq_count)
    seq_segments = split_seqs(segments, seq_count)
    attended, log_total = lax.map(attend, (seq_queries, seq_keys, seq_values, seq_segments))
    attended_low = attended.reshape(row_count, D)
    residual = hidden_in + jnp.dot(attended_low, out_low, preferred_element_type=jnp.float32)
    normed_two, norm_back_two = jax.vjp(layer_norm, residual, gains_full[1])
    normed_two_low = normed_two.astype(jnp.bfloat16)
    gate_up = jnp.dot(normed_two_low, in_low, preferred_element_type=jnp.float32)
    active, geglu_back = jax.vjp(geglu, gate_up)
    active_low = active.astype(jnp.bfloat16)
    output = residual + jnp.dot(active_low, down_low, preferred_element_type=jnp.float32)
    activations = output.astype(jnp.bfloat16)
    gathered_back = (
        lax.all_gather(rounded[0], "fsdp", axis=0, tiled=True),
        lax.all_gather(rounded[1], "fsdp", axis=0, tiled=True),
        lax.all_gather(rounded[2], "fsdp", axis=0, tiled=True),
        lax.all_gather(rounded[3], "fsdp", axis=0, tiled=True),
        lax.all_gather(rounded[4], "fsdp", axis=1, tiled=True),
    )
    qkv_low, out_low, in_low, down_low, gains_low = gathered_back
    grad_down = jnp.dot(active_low.T, cotangent, preferred_element_type=jnp.float32)
    grad_active = jnp.dot(cotangent, down_low.T, preferred_element_type=jnp.float32)
    grad_gate_up = geglu_back(grad_active)[0].astype(jnp.bfloat16)
    grad_in = jnp.dot(normed_two_low.T, grad_gate_up, preferred_element_type=jnp.float32)
    grad_normed_two = jnp.dot(grad_gate_up, in_low.T, preferred_element_type=jnp.float32)
    grad_resid_norm, gain_two_grad = norm_back_two(grad_normed_two)
    grad_residual = cotangent.astype(jnp.float32) + grad_resid_norm
    grad_residual_low = grad_residual.astype(jnp.bfloat16)
    grad_outw = jnp.dot(attended_low.T, grad_residual_low, preferred_element_type=jnp.float32)
    grad_attended = jnp.dot(
        grad_residual_low, out_low.T, preferred_element_type=jnp.float32
    ).astype(jnp.bfloat16)
    seq_grad_heads = split_seqs(grad_attended.reshape(row_count, HEADS, HEAD), seq_count)
    grad_queries, grad_keys, grad_values = lax.map(
        attend_back, (seq_queries, seq_keys, seq_values, seq_grad_heads, log_total, seq_segments)
    )
    grad_queries = rotate(grad_queries.reshape(row_count, HEADS, HEAD), cosine, -sine)
    grad_keys = rotate(grad_keys.reshape(row_count, HEADS, HEAD), cosine, -sine)
    grad_mixed = jnp.concatenate(
        [
            grad_queries.reshape(row_count, D),
            grad_keys.reshape(row_count, D),
            grad_values.reshape(row_count, D),
        ],
        axis=1,
    ).astype(jnp.bfloat16)
    grad_qkv = jnp.dot(normed_low.T, grad_mixed, preferred_element_type=jnp.float32)
    grad_normed = jnp.dot(grad_mixed, qkv_low.T, preferred_element_type=jnp.float32)
    grad_input_norm, gain_one_grad = norm_back_one(grad_normed)
    input_grad = grad_residual + grad_input_norm
    gain_pair_grad = jnp.stack([gain_one_grad, gain_two_grad])
    owned_qkv, owned_out, owned_in, owned_down, owned_gain = (
        lax.psum_scatter(grad_qkv, "fsdp", scatter_dimension=0, tiled=True),
        lax.psum_scatter(grad_outw, "fsdp", scatter_dimension=0, tiled=True),
        lax.psum_scatter(grad_in, "fsdp", scatter_dimension=0, tiled=True),
        lax.psum_scatter(grad_down, "fsdp", scatter_dimension=0, tiled=True),
        lax.psum_scatter(gain_pair_grad, "fsdp", scatter_dimension=1, tiled=True),
    )
    qkv_state = adam_step(qkv_weight, owned_qkv, qkv_first, qkv_second)
    out_state = adam_step(out_weight, owned_out, out_first, out_second)
    in_state = adam_step(in_weight, owned_in, in_first, in_second)
    down_state = adam_step(down_weight, owned_down, down_first, down_second)
    gains_state = adam_step(norm_gains, owned_gain, gains_first, gains_second)
    gains_delta = gains_state[1] - norm_gains
    return (
        activations,
        input_grad,
        qkv_state[0],
        qkv_state[1],
        qkv_state[2],
        qkv_state[3],
        out_state[0],
        out_state[1],
        out_state[2],
        out_state[3],
        in_state[0],
        in_state[1],
        in_state[2],
        in_state[3],
        down_state[0],
        down_state[1],
        down_state[2],
        down_state[3],
        gains_state[0],
        gains_delta,
        gains_state[2],
        gains_state[3],
    )


def solution(mesh):
    return jax.shard_map(
        shards,
        mesh=mesh,
        in_specs=(
            P("fsdp", None),
            P("fsdp", None),
            P("fsdp"),
            P("fsdp"),
            P("fsdp", None),
            P("fsdp", None),
            P("fsdp", None),
            P("fsdp", None),
            P("fsdp", None),
            P("fsdp", None),
            P("fsdp", None),
            P("fsdp", None),
            P("fsdp", None),
            P("fsdp", None),
            P("fsdp", None),
            P("fsdp", None),
            P(None, "fsdp"),
            P(None, "fsdp"),
            P(None, "fsdp"),
        ),
        out_specs=(
            P("fsdp", None),
            P("fsdp", None),
            P("fsdp", None),
            P("fsdp", None),
            P("fsdp", None),
            P("fsdp", None),
            P("fsdp", None),
            P("fsdp", None),
            P("fsdp", None),
            P("fsdp", None),
            P("fsdp", None),
            P("fsdp", None),
            P("fsdp", None),
            P("fsdp", None),
            P("fsdp", None),
            P("fsdp", None),
            P("fsdp", None),
            P("fsdp", None),
            P(None, "fsdp"),
            P(None, "fsdp"),
            P(None, "fsdp"),
            P(None, "fsdp"),
        ),
        check_vma=False,
    )
```

profile of v0, /device:TPU:0, one launch (start us, length us, event | category | flops | bytes accessed | tf_op | source)
XLA Modules:
  0.0 1512.9 jit_solution(8953548538941148751)
XLA Ops:
  18.5 43.1 %all-gather = bf16[32,24,2]{1,2,0:T(2,128)(2,1)S(1)} all-gather(bf16[1,24,2]{1,2,0:T(2,128)(2,1)S(1)} %convert_bitcast_fusion.1), channel_id=1, replica_groups=mesh['fsdp'=32] {'fsdp'}, dimensions={0}, use_global_device_ids=true | all-gather | bytes 3168 | tf_op jit(solution)/shard_map/all_gather | solution.py:177
  75.7 57.1 %all-gather.7.cloned.1.call-done = bf16[768,2304]{1,0:T(8,128)(2,1)} async-done(((bf16[24,2304]{1,0:T(8,128)(2,1)}), bf16[768,2304]{1,0:T(8,128)(2,1)}) %all-gather.7.cloned.1.call-update) | async-done | bytes 3538960 | tf_op jit(solution)/shard_map/all_gather | solution.py:173
  132.8 13.6 fusion.103
  146.4 10.2 fusion.135
  159.7 6.6 copy.175
  166.3 8.4 reshape.589
  174.7 6.5 slice_negate_fusion.3
  191.7 6.6 copy.177
  198.4 8.4 reshape.591
  206.8 6.4 slice_negate_fusion.2
  213.2 5.6 concatenate.185
  218.8 5.3 concatenate.186
  224.1 10.3 fusion.94
  242.1 6.1 convert_element_type.113
  250.9 250.1 %while.30 = (s32[]{:T(128)}, bf16[4,512,12,64]{1,3,2,0:T(8,128)(2,1)}, f32[4,4,12,128,1]{3,2,1,4,0:T(8,128)}, bf16[4,512,12,64]{1,3,2,0:T(8,128)(2,1)S(1)}, s32[...) while((s32[]{:T(128)}, ...), condition=%wide.region_5.6_spmd, body=%wide.region_2.5_spmd.sunk | while | flops 657465344 | bytes 106623328 | solution.py:199
  301.4 6.1 fusion.187
  363.9 6.1 fusion.187
  426.4 6.1 fusion.187
  488.8 6.1 fusion.187
  501.0 5.5 copy.182
  509.2 6.0 fusion.136
  518.7 11.3 fusion.121
  530.0 26.2 %fusion.98 = (f32[2048,1152]{1,0:T(8,128)}, f32[2048,1152]{1,0:T(8,128)}, f32[2048,1152]{1,0:T(8,128)}) fusion(f32[2048,2304]{1,0:T(8,128)S(1)} %fusion.121, bf16[2048,768]{1,0:T(8,128)(2,1)S(1)} %copy-done.19, bf16[1152,768]{1,0:T(8,128)(2,1)S(1)} %copy-done.25), kind=kOutput, calls=%fused_computation.188 | convolution fusion | flops 3777232896 | bytes 42663936 | tf_op jit(solution)/shard_map/dot_general | solution.py:218
  556.2 14.6 multiply_add_fusion
  570.7 16.2 %multiply_reduce_fusion.1 = (f32[768]{0:T(1024)}, f32[2048]{0:T(1024)S(1)}, f32[2048,768]{0,1:T(8,128)}) fusion(f32[2048,768]{0,1:T(8,128)} %copy-done.10, f32[2048]{0:T(1024)S(1)} %fusion.115, f32[2048]{0:T(1024)S(1)} %broadcast_multiply_fusion.2, f32[768]{0:T(1024)S(1)} %copy-done.41, bf16[768,2304]{1,0:T(8,128)(2,1)} %all-gather.11.cloned.1.call-done, ...), kind=kOutput, calls=%fused_computation.173 | convolution fusion | flops 7268201472 | bytes 35026944 | tf_op jit(solution)/shard_map/dot_general | solution.py:221
  587.0 5.8 fusion.127
  604.3 5.3 convolution_convert_fusion
  621.2 19.0 %fusion.99 = f32[768,2304]{1,0:T(8,128)} fusion(f32[2048,1152]{1,0:T(8,128)} %get-tuple-element.515, f32[2048,1152]{1,0:T(8,128)} %get-tuple-element.463, f32[2048,768]{0,1:T(8,128)} %copy-done.10, f32[768]{0:T(1024)S(1)} %copy-done.41, f32[2048]{0:T(1024)S(1)} %fusion.115, f32[2048]{0:T(1024)S(1)} %broadcast_multiply_fusion.2), kind=kOutput, calls=%fused_computation.189 | convolution fusion | flops 7263485952 | bytes 32263168 | tf_op jit(solution)/shard_map/dot_general | solution.py:220
  642.0 588.1 %while.31 = (s32[]{:T(128)}, f32[4,512,12,64]{1,0,3,2:T(4,128)}, f32[4,512,12,64]{1,0,3,2:T(4,128)}, bf16[4,512,12,64]{1,3,2,0:T(8,128)(2,1)}, bf16[4,512,12,64]...) while((s32[]{:T(128)}, f32[4,512,12,64]{1,0,3,2:T(4,128)}, ...), condition=%wide.region_12.13_spmd, body=%wide.region_10.12_spmd.sunk | while | flops 1587027968 | bytes 218263584 | solution.py:230
  666.4 6.8 fusion.194
  679.7 5.4 fusion.201
  705.2 6.7 multiply_reduce_fusion.5
  719.8 31.3 %dynamic_update_slice.45 = f32[4,512,12,64]{1,0,3,2:T(4,128)} dynamic-update-slice(f32[4,512,12,64]{1,0,3,2:T(4,128)} %get-tuple-element.790, f32[1,512,12,64]{1,0,3,2:T(1,128)} %bitcast.205, s32[]{:T(128)} %get-tuple-element.788, s32[]{:T(128)} %constant.218.clone.1..sunk.1, s32[]{:T(128)} %constant.218.clone.1..sunk.1, s32[]{:T(128)} %constant.218.clone.1..sunk.1) | dynamic-update-slice | bytes 3145732 | tf_op jit(solution)/shard_map/while/body/jit(dynamic_update_index_in_dim)/dynamic_update_slice | solution.py:230
  758.4 31.2 %dynamic_update_slice.44 = f32[4,512,12,64]{1,0,3,2:T(4,128)} dynamic-update-slice(f32[4,512,12,64]{1,0,3,2:T(4,128)} %get-tuple-element.789, f32[1,512,12,64]{1,0,3,2:T(1,128)} %bitcast.204, s32[]{:T(128)} %get-tuple-element.788, s32[]{:T(128)} %constant.218.clone.1..sunk.1, s32[]{:T(128)} %constant.218.clone.1..sunk.1, s32[]{:T(128)} %constant.218.clone.1..sunk.1) | dynamic-update-slice | bytes 3145732 | tf_op jit(solution)/shard_map/while/body/jit(dynamic_update_index_in_dim)/dynamic_update_slice | solution.py:230
  813.5 6.8 fusion.194
  826.8 5.3 fusion.201
  852.3 6.7 multiply_reduce_fusion.5
  866.9 31.0 %dynamic_update_slice.45 = f32[4,512,12,64]{1,0,3,2:T(4,128)} dynamic-update-slice(f32[4,512,12,64]{1,0,3,2:T(4,128)} %get-tuple-element.790, f32[1,512,12,64]{1,0,3,2:T(1,128)} %bitcast.205, s32[]{:T(128)} %get-tuple-element.788, s32[]{:T(128)} %constant.218.clone.1..sunk.1, s32[]{:T(128)} %constant.218.clone.1..sunk.1, s32[]{:T(128)} %constant.218.clone.1..sunk.1) | dynamic-update-slice | bytes 3145732 | tf_op jit(solution)/shard_map/while/body/jit(dynamic_update_index_in_dim)/dynamic_update_slice | solution.py:230
  905.3 31.0 %dynamic_update_slice.44 = f32[4,512,12,64]{1,0,3,2:T(4,128)} dynamic-update-slice(f32[4,512,12,64]{1,0,3,2:T(4,128)} %get-tuple-element.789, f32[1,512,12,64]{1,0,3,2:T(1,128)} %bitcast.204, s32[]{:T(128)} %get-tuple-element.788, s32[]{:T(128)} %constant.218.clone.1..sunk.1, s32[]{:T(128)} %constant.218.clone.1..sunk.1, s32[]{:T(128)} %constant.218.clone.1..sunk.1) | dynamic-update-slice | bytes 3145732 | tf_op jit(solution)/shard_map/while/body/jit(dynamic_update_index_in_dim)/dynamic_update_slice | solution.py:230
  960.3 6.8 fusion.194
  973.5 5.3 fusion.201
  999.1 6.7 multiply_reduce_fusion.5
  1013.7 31.0 %dynamic_update_slice.45 = f32[4,512,12,64]{1,0,3,2:T(4,128)} dynamic-update-slice(f32[4,512,12,64]{1,0,3,2:T(4,128)} %get-tuple-element.790, f32[1,512,12,64]{1,0,3,2:T(1,128)} %bitcast.205, s32[]{:T(128)} %get-tuple-element.788, s32[]{:T(128)} %constant.218.clone.1..sunk.1, s32[]{:T(128)} %constant.218.clone.1..sunk.1, s32[]{:T(128)} %constant.218.clone.1..sunk.1) | dynamic-update-slice | bytes 3145732 | tf_op jit(solution)/shard_map/while/body/jit(dynamic_update_index_in_dim)/dynamic_update_slice | solution.py:230
  1052.1 31.0 %dynamic_update_slice.44 = f32[4,512,12,64]{1,0,3,2:T(4,128)} dynamic-update-slice(f32[4,512,12,64]{1,0,3,2:T(4,128)} %get-tuple-element.789, f32[1,512,12,64]{1,0,3,2:T(1,128)} %bitcast.204, s32[]{:T(128)} %get-tuple-element.788, s32[]{:T(128)} %constant.218.clone.1..sunk.1, s32[]{:T(128)} %constant.218.clone.1..sunk.1, s32[]{:T(128)} %constant.218.clone.1..sunk.1) | dynamic-update-slice | bytes 3145732 | tf_op jit(solution)/shard_map/while/body/jit(dynamic_update_index_in_dim)/dynamic_update_slice | solution.py:230
  1107.0 6.8 fusion.194
  1120.3 5.3 fusion.201
  1145.8 6.7 multiply_reduce_fusion.5
  1160.4 31.0 %dynamic_update_slice.45 = f32[4,512,12,64]{1,0,3,2:T(4,128)} dynamic-update-slice(f32[4,512,12,64]{1,0,3,2:T(4,128)} %get-tuple-element.790, f32[1,512,12,64]{1,0,3,2:T(1,128)} %bitcast.205, s32[]{:T(128)} %get-tuple-element.788, s32[]{:T(128)} %constant.218.clone.1..sunk.1, s32[]{:T(128)} %constant.218.clone.1..sunk.1, s32[]{:T(128)} %constant.218.clone.1..sunk.1) | dynamic-update-slice | bytes 3145732 | tf_op jit(solution)/shard_map/while/body/jit(dynamic_update_index_in_dim)/dynamic_update_slice | solution.py:230
  1198.7 31.0 %dynamic_update_slice.44 = f32[4,512,12,64]{1,0,3,2:T(4,128)} dynamic-update-slice(f32[4,512,12,64]{1,0,3,2:T(4,128)} %get-tuple-element.789, f32[1,512,12,64]{1,0,3,2:T(1,128)} %bitcast.204, s32[]{:T(128)} %get-tuple-element.788, s32[]{:T(128)} %constant.218.clone.1..sunk.1, s32[]{:T(128)} %constant.218.clone.1..sunk.1, s32[]{:T(128)} %constant.218.clone.1..sunk.1) | dynamic-update-slice | bytes 3145732 | tf_op jit(solution)/shard_map/while/body/jit(dynamic_update_index_in_dim)/dynamic_update_slice | solution.py:230
  1230.2 8.5 reshape.595
  1238.7 8.6 reshape.597
  1247.3 8.7 copy.217
  1256.0 5.7 copy.218
  1266.9 9.3 slice_negate_fusion
  1276.1 6.6 maximum_multiply_fusion.2
  1282.8 8.5 fusion.88
  1291.3 14.2 fusion.96
  1305.6 9.1 fusion.138
  1314.7 89.5 %fusion = f32[40,768]{1,0:T(8,128)S(1)} fusion(f32[1152,768]{1,0:T(8,128)} %fusion.138), kind=kCustom, calls=%all-reduce-scatter | all-reduce-scatter fusion | flops 983041 | bytes 3661824
  1410.0 11.3 fusion.86
  1428.5 38.5 %all-reduce.3 = f32[2,768]{1,0:T(2,128)S(1)} all-reduce(f32[2,768]{1,0:T(2,128)S(1)} %pad_maximum_fusion.5), channel_id=6, replica_groups=mesh['fsdp'=32] {'fsdp'}, use_global_device_ids=true, to_apply=%region_21.22.clone | all-reduce | flops 1536 | bytes 12288
  1467.0 10.8 add_convert_fusion.1
  1477.8 6.7 add_add_fusion.4
  1485.3 6.7 copy.196
  (581 shorter events, 600.2 us)
Async XLA Ops:
  7.2 64.9 %all-gather.13.cloned.1.call-start = ((), (), s32[]{:S(2)}) async-start(), calls=%async_computation.9 | async-start | bytes 2027520 | tf_op jit(solution)/shard_map/all_gather | solution.py:176
  8.8 123.9 %all-gather.7.cloned.1.call-start = ((), (), s32[]{:S(2)}) async-start(), calls=%async_computation.3 | async-start | bytes 3649536 | tf_op jit(solution)/shard_map/all_gather | solution.py:173
  10.5 498.7 %all-gather.9.cloned.1.call-start = ((), (), s32[]{:S(2)}) async-start(), calls=%async_computation.4 | async-start | bytes 1216512 | tf_op jit(solution)/shard_map/all_gather | solution.py:174
  12.0 506.6 %all-gather.11.cloned.1.call-start = ((), (), s32[]{:S(2)}) async-start(), calls=%async_computation.5 | async-start | bytes 3649536 | tf_op jit(solution)/shard_map/all_gather | solution.py:175
  13.7 1486.1 %reduce-scatter.9.cloned.1.call-start = ((), (), s32[]{:S(2)}) async-start(), calls=%async_computation.7 | async-start | bytes 2433024 | tf_op jit(solution)/shard_map/reduce_scatter | solution.py:250
  13.8 48.7 %copy-start.45 = (f32[32]{0:T(128)}, f32[32]{0:T(128)S(1)}, u32[]{:S(2)}) copy-start(f32[32]{0:T(128)S(1)} %negate_power_fusion) | copy-start | bytes 388
  13.9 48.6 %copy-start.42 = (s32[2048]{0:T(1024)S(1)}, s32[2048]{0:T(1024)}, u32[]{:S(2)}) copy-start(s32[2048]{0:T(1024)} %param.26) | copy-start | bytes 24580
  13.9 53.4 %copy-start.43 = (s32[2048]{0:T(1024)S(1)}, s32[2048]{0:T(1024)}, u32[]{:S(2)}) copy-start(s32[2048]{0:T(1024)} %param.25) | copy-start | bytes 24580
  17.1 115.7 %copy-start.5 = (bf16[2048,768]{0,1:T(8,128)(2,1)}, bf16[2048,768]{0,1:T(8,128)(2,1)S(1)}, u32[]{:S(2)}) copy-start(bf16[2048,768]{0,1:T(8,128)(2,1)S(1)} %copy.171) | copy-start | bytes 9437188
  17.6 115.2 %copy-start.29 = (f32[2048]{0:T(1024)}, f32[2048]{0:T(1024)S(1)}, u32[]{:S(2)}) copy-start(f32[2048]{0:T(1024)S(1)} %broadcast_multiply_fusion.3) | copy-start | bytes 24580
  18.5 43.1 %copy-start.35 = (f32[2048]{0:T(1024)}, f32[2048]{0:T(1024)S(1)}, u32[]{:S(2)}) copy-start(f32[2048]{0:T(1024)S(1)} %fusion.85) | copy-start | bytes 24580
  18.5 127.9 %copy-start.31 = (f32[2048]{0:T(1024)}, f32[2048]{0:T(1024)S(1)}, u32[]{:S(2)}) copy-start(f32[2048]{0:T(1024)S(1)} %fusion.114) | copy-start | bytes 24580
  62.5 83.9 %copy-start.39 = (f32[768]{0:T(1024)}, f32[768]{0:T(1024)S(1)}, u32[]{:S(2)}) copy-start(f32[768]{0:T(1024)S(1)} %get-tuple-element.409) | copy-start | bytes 9220
  62.5 83.9 %copy-start.37 = (f32[2048]{0:T(1024)}, f32[2048]{0:T(1024)S(1)}, u32[]{:S(2)}) copy-start(f32[2048]{0:T(1024)S(1)} %convert_element_type.114) | copy-start | bytes 24580
  279.7 6.9 copy-start.17
  342.1 6.9 copy-start.17
  404.6 6.9 copy-start.17
  467.0 6.9 copy-start.17
  501.0 8.2 copy-start.2
  501.0 8.2 copy-start.27
  518.6 11.3 copy-start.19
  518.7 11.3 copy-start.25
  601.0 900.5 %reduce-scatter.11.cloned.1.call-start = ((), (), s32[]{:S(2)}) async-start(), calls=%async_computation.8 | async-start | bytes 7299072 | tf_op jit(solution)/shard_map/reduce_scatter | solution.py:251
  640.2 863.4 %reduce-scatter.7.cloned.1.call-start = ((), (), s32[]{:S(2)}) async-start(), calls=%async_computation.6 | async-start | bytes 7299072 | tf_op jit(solution)/shard_map/reduce_scatter | solution.py:249
  656.5 16.7 %copy-start.13 = (bf16[1,128,12,64]{1,3,2,0:T(8,128)(2,1)}, bf16[1,128,12,64]{1,3,2,0:T(8,128)(2,1)S(1)}, u32[]{:S(2)}) copy-start(bf16[1,128,12,64]{1,3,2,0:T(8,128)(2,1)S(1)} %get-tuple-element.714) | copy-start | bytes 589828 | tf_op jit(solution)/shard_map/while
  703.7 8.3 slice-start
  705.2 6.8 slice-start.1
  705.2 6.8 slice-start.2
  705.2 6.8 copy-start.16
  717.1 33.9 %copy-start.14 = (bf16[1,128,12,64]{1,3,2,0:T(8,128)(2,1)S(1)}, bf16[1,128,12,64]{1,3,2,0:T(8,128)(2,1)}, u32[]{:S(2)}) copy-start(bf16[1,128,12,64]{1,3,2,0:T(8,128)(2,1)} %copy-done.13) | copy-start | bytes 589828 | tf_op jit(solution)/shard_map/while
  803.7 16.6 %copy-start.13 = (bf16[1,128,12,64]{1,3,2,0:T(8,128)(2,1)}, bf16[1,128,12,64]{1,3,2,0:T(8,128)(2,1)S(1)}, u32[]{:S(2)}) copy-start(bf16[1,128,12,64]{1,3,2,0:T(8,128)(2,1)S(1)} %get-tuple-element.714) | copy-start | bytes 589828 | tf_op jit(solution)/shard_map/while
  850.8 8.3 slice-start
  852.3 6.8 slice-start.1
  852.3 6.8 slice-start.2
  852.3 6.8 copy-start.16
  864.2 33.7 %copy-start.14 = (bf16[1,128,12,64]{1,3,2,0:T(8,128)(2,1)S(1)}, bf16[1,128,12,64]{1,3,2,0:T(8,128)(2,1)}, u32[]{:S(2)}) copy-start(bf16[1,128,12,64]{1,3,2,0:T(8,128)(2,1)} %copy-done.13) | copy-start | bytes 589828 | tf_op jit(solution)/shard_map/while
  950.5 16.6 %copy-start.13 = (bf16[1,128,12,64]{1,3,2,0:T(8,128)(2,1)}, bf16[1,128,12,64]{1,3,2,0:T(8,128)(2,1)S(1)}, u32[]{:S(2)}) copy-start(bf16[1,128,12,64]{1,3,2,0:T(8,128)(2,1)S(1)} %get-tuple-element.714) | copy-start | bytes 589828 | tf_op jit(solution)/shard_map/while
  997.6 8.3 slice-start
  999.1 6.8 slice-start.1
  999.1 6.8 slice-start.2
  999.1 6.8 copy-start.16
  1011.0 33.7 %copy-start.14 = (bf16[1,128,12,64]{1,3,2,0:T(8,128)(2,1)S(1)}, bf16[1,128,12,64]{1,3,2,0:T(8,128)(2,1)}, u32[]{:S(2)}) copy-start(bf16[1,128,12,64]{1,3,2,0:T(8,128)(2,1)} %copy-done.13) | copy-start | bytes 589828 | tf_op jit(solution)/shard_map/while
  1097.2 16.6 %copy-start.13 = (bf16[1,128,12,64]{1,3,2,0:T(8,128)(2,1)}, bf16[1,128,12,64]{1,3,2,0:T(8,128)(2,1)S(1)}, u32[]{:S(2)}) copy-start(bf16[1,128,12,64]{1,3,2,0:T(8,128)(2,1)S(1)} %get-tuple-element.714) | copy-start | bytes 589828 | tf_op jit(solution)/shard_map/while
  1144.3 8.3 slice-start
  1145.8 6.8 slice-start.1
  1145.8 6.8 slice-start.2
  1157.7 33.7 %copy-start.14 = (bf16[1,128,12,64]{1,3,2,0:T(8,128)(2,1)S(1)}, bf16[1,128,12,64]{1,3,2,0:T(8,128)(2,1)}, u32[]{:S(2)}) copy-start(bf16[1,128,12,64]{1,3,2,0:T(8,128)(2,1)} %copy-done.13) | copy-start | bytes 589828 | tf_op jit(solution)/shard_map/while
  1238.7 17.3 %slice-start.3 = ((s8[6291456]{0:T(1024)(128)(4,1)}), s8[2097152]{0:T(1024)(128)(4,1)S(1)}, s32[]{:S(2)}) async-start(s8[6291456]{0:T(1024)(128)(4,1)} %bitcast.209), calls=%async_computation.13 | async-start | bytes 4194304
  1247.3 8.7 slice-start.4
  1266.9 9.3 copy-start.24
  1266.9 15.9 %slice-start.5 = ((s8[6291456]{0:T(1024)(128)(4,1)}), s8[2097152]{0:T(1024)(128)(4,1)S(1)}, s32[]{:S(2)}) async-start(s8[6291456]{0:T(1024)(128)(4,1)} %bitcast.212), calls=%async_computation.15 | async-start | bytes 4194304
  1282.8 8.5 copy-start.6
  1282.8 8.5 copy-start.30
  1282.8 8.5 copy-start.32
  1282.8 8.5 copy-start.40
  1404.2 90.6 %collective-permute-start = (f32[40,768]{1,0:T(8,128)S(1)}, f32[40,768]{1,0:T(8,128)}, u32[]{:S(2)}, u32[]{:S(2)}) collective-permute-start(f32[40,768]{1,0:T(8,128)S(1)} %fusion), channel_id=1, source_target_pairs={{0,1},{1,2},{2,3},{3,4},{4,5},{5,6},{6,7},{7,8},{8,9},{9,10},{10,1... | collective-permute-start | bytes 368648
  1406.1 88.6 %collective-permute-start.1 = (f32[40,768]{1,0:T(8,128)S(1)}, f32[40,768]{1,0:T(8,128)}, u32[]{:S(2)}, u32[]{:S(2)}) collective-permute-start(f32[40,768]{1,0:T(8,128)S(1)} %fusion), channel_id=1, source_target_pairs={{0,2},{1,3},{2,4},{3,5},{4,6},{5,7},{6,8},{7,9},{8,10},{9,11},{10,... | collective-permute-start | bytes 368648
  1408.1 86.7 %collective-permute-start.2 = (f32[40,768]{1,0:T(8,128)S(1)}, f32[40,768]{1,0:T(8,128)}, u32[]{:S(2)}, u32[]{:S(2)}) collective-permute-start(f32[40,768]{1,0:T(8,128)S(1)} %fusion), channel_id=1, source_target_pairs={{0,3},{1,4},{2,5},{3,6},{4,7},{5,8},{6,9},{7,10},{8,11},{9,12},{10... | collective-permute-start | bytes 368648
  1410.0 11.3 copy-start.36
  1427.2 67.6 %collective-permute-start.3 = (f32[4,768]{1,0:T(4,128)S(1)}, f32[4,768]{1,0:T(4,128)S(1)}, u32[]{:S(2)}, u32[]{:S(2)}) collective-permute-start(f32[4,768]{1,0:T(4,128)S(1)} %slice.362), channel_id=1, source_target_pairs={{0,4},{1,5},{2,6},{3,7},{4,8},{5,9},{6,10},{7,11},{8,12},{9,13},{1... | collective-permute-start | bytes 36872
  1467.0 10.8 copy-start.9
  1467.0 10.8 copy-start.12
  1467.0 10.8 copy-start.34
  1492.0 9.5 copy-start.26
  (41 other events, 159.3 us)
Sparse Core Ops, SparseCore 0:
  11.5 58.8 all-gather.12
  73.8 58.8 all-gather.6
  136.2 52.8 all-gather.8
  192.4 59.0 all-gather.10
  601.1 97.8 reduce-scatter.8
  706.1 118.0 reduce-scatter.10
  1305.7 133.9 reduce-scatter.6
where the time goes:
time: 1530 us; the launch traced here: 1510 us
  local copies, waits for them, and re-layouts  834 us (55%)
  matrix products  287 us (19%)
  blocking collectives  171 us (11%)
  other arithmetic  139 us (9%)
  waiting for transfers between devices  57.2 us (4%)
    dynamic_update_slice x12, local copies, waits for them, and re-layouts, shards(): lax.map(attend_back, (seq_queries, seq_keys, seq_values, seq_grad_heads,...  257 us
    unnamed x2, blocking collectives  128 us
    slice x64, local copies, waits for them, and re-layouts, widen(): before = jnp.roll(blocked, 1, axis=0)  115 us
    slice x32, local copies, waits for them, and re-layouts, widen(): after = jnp.roll(blocked, -1, axis=0)  76 us
    all_gather x1, waiting for transfers between devices, shards(): lax.all_gather(rounded[0], 'fsdp', axis=0, tiled=True)  57.1 us
    unnamed x103, local copies, waits for them, and re-layouts  54.2 us
    all_gather x1, blocking collectives, shards(): lax.all_gather(rounded[4], 'fsdp', axis=1, tiled=True)  43.1 us
    dot_general x8, matrix products, block_scores(): jnp.einsum('bqhe,bkhe->bhqk', query_blocks, key_wide, preferred_element_t...  42.9 us
  transfers between devices with their start and end apart: 11, of which 1 were waited for; matrix products, arithmetic and copies ran while one was open for 82% of the time, Pallas kernels for 0%

commit v1 on v0

--- a/solution.py
+++ b/solution.py
@@ -174,7 +174,9 @@
         lax.all_gather(rounded[1], "fsdp", axis=0, tiled=True),
         lax.all_gather(rounded[2], "fsdp", axis=0, tiled=True),
         lax.all_gather(rounded[3], "fsdp", axis=0, tiled=True),
-        lax.all_gather(rounded[4], "fsdp", axis=1, tiled=True),
+        jnp.concatenate(
+            lax.all_to_all(jnp.stack([rounded[4]] * lax.axis_size("fsdp")), "fsdp", 0, 0), axis=1
+        ),
     )
     qkv_low, out_low, in_low, down_low, gains_low = gathered
     gains_full = gains_low.astype(jnp.float32)

time: 1530 us -> 1540 us (level)
  blocking collectives: 171 us -> 128 us
  waiting for transfers between devices: 57.2 us -> 91.8 us
    all_gather x1 -> x0, blocking collectives: 43.1 us -> none  [shards(): lax.all_gather(rounded[4], 'fsdp', axis=1, tiled=True)]
    all_gather x1, waiting for transfers between devices: 0.01 us -> 32.9 us  [shards(): lax.all_gather(rounded[3], 'fsdp', axis=0, tiled=True)]
    unnamed x103 -> x101, local copies, waits for them, and re-layouts: 54.2 us -> 57.7 us
  transfers between devices with their start and end apart: 11 -> 12, of which waited for: 1 -> 2; matrix products, arithmetic and copies ran while one was open for 82% -> 82% of each run, Pallas kernels for 0% -> 0%
where the time goes in v1:
time: 1540 us; the launch traced here: 1520 us
  local copies, waits for them, and re-layouts  838 us (54%)
  matrix products  289 us (19%)
  other arithmetic  140 us (9%)
  blocking collectives  128 us (8%)
  waiting for transfers between devices  91.8 us (6%)
    dynamic_update_slice x12, local copies, waits for them, and re-layouts, shards(): lax.map(attend_back, (seq_queries, seq_keys, seq_values, seq_grad_heads,...  257 us
    unnamed x2, blocking collectives  128 us
    slice x64, local copies, waits for them, and re-layouts, widen(): before = jnp.roll(blocked, 1, axis=0)  115 us
    slice x32, local copies, waits for them, and re-layouts, widen(): after = jnp.roll(blocked, -1, axis=0)  75.6 us
    all_gather x1, waiting for transfers between devices, shards(): lax.all_gather(rounded[0], 'fsdp', axis=0, tiled=True)  58.7 us
    unnamed x101, local copies, waits for them, and re-layouts  57.7 us
    dot_general x8, matrix products, block_scores(): jnp.einsum('bqhe,bkhe->bhqk', query_blocks, key_wide, preferred_element_t...  43 us
    reshape x16, local copies, waits for them, and re-layouts, block_scores(): key_wide = widen(key_heads.reshape(block_count, BLK, HEADS, HEAD))  37.3 us
  transfers between devices with their start and end apart: 12, of which 2 were waited for; matrix products, arithmetic and copies ran while one was open for 82% of the time, Pallas kernels for 0%

profile of v1, /device:TPU:0, one launch (start us, length us, event | category | flops | bytes accessed | tf_op | source)
XLA Modules:
  0.0 1518.3 jit_solution(11908365666583091359)
XLA Ops:
  13.3 7.3 all-to-all-start
  37.4 32.9 %all-gather.12.cloned.1.call-done = bf16[32,36,768]{2,1,0:T(8,128)(2,1)} async-done(((bf16[1,36,768]{2,1,0:T(8,128)(2,1)}), bf16[32,36,768]{2,1,0:T(8,128)(2,1)}) %all-gather.12.cloned.1.call-update) | async-done | bytes 1769488 | tf_op jit(solution)/shard_map/all_gather | solution.py:176
  74.0 58.7 %all-gather.6.cloned.1.call-done = bf16[768,2304]{1,0:T(8,128)(2,1)} async-done(((bf16[24,2304]{1,0:T(8,128)(2,1)}), bf16[768,2304]{1,0:T(8,128)(2,1)}) %all-gather.6.cloned.1.call-update) | async-done | bytes 3538960 | tf_op jit(solution)/shard_map/all_gather | solution.py:173
  132.7 13.7 fusion.103
  146.4 10.2 fusion.135
  159.7 6.7 copy.126
  166.3 8.4 reshape.598
  174.8 6.5 slice_negate_fusion.3
  191.8 6.8 copy.128
  198.6 8.4 reshape.600
  207.1 6.4 slice_negate_fusion.2
  213.5 5.3 concatenate.185
  224.0 10.3 fusion.94
  241.9 6.2 convert_element_type.118
  250.8 250.6 %while.30 = (s32[]{:T(128)}, bf16[4,512,12,64]{1,3,2,0:T(8,128)(2,1)}, f32[4,4,12,128,1]{3,2,1,4,0:T(8,128)}, bf16[4,512,12,64]{1,3,2,0:T(8,128)(2,1)S(1)}, s32[...) while((s32[]{:T(128)}, ...), condition=%wide.region_5.6_spmd, body=%wide.region_2.5_spmd.sunk | while | flops 657465344 | bytes 106623328 | solution.py:201
  301.7 6.1 fusion.187
  364.2 6.1 fusion.187
  426.7 6.1 fusion.187
  489.2 6.1 fusion.187
  501.5 5.5 copy.133
  509.6 6.0 fusion.136
  519.1 11.3 fusion.121
  530.4 26.1 %fusion.98 = (f32[2048,1152]{1,0:T(8,128)}, f32[2048,1152]{1,0:T(8,128)}, f32[2048,1152]{1,0:T(8,128)}) fusion(f32[2048,2304]{1,0:T(8,128)S(1)} %fusion.121, bf16[2048,768]{1,0:T(8,128)(2,1)S(1)} %copy-done.19, bf16[1152,768]{1,0:T(8,128)(2,1)S(1)} %copy-done.26), kind=kOutput, calls=%fused_computation.188 | convolution fusion | flops 3777232896 | bytes 42663936 | tf_op jit(solution)/shard_map/dot_general | solution.py:220
  556.5 14.6 multiply_add_fusion
  571.1 16.3 %multiply_reduce_fusion.1 = (f32[768]{0:T(1024)}, f32[2048]{0:T(1024)S(1)}, f32[2048,768]{0,1:T(8,128)}) fusion(f32[2048,768]{0,1:T(8,128)} %copy-done.10, f32[2048]{0:T(1024)S(1)} %fusion.115, f32[2048]{0:T(1024)S(1)} %broadcast_multiply_fusion.2, f32[768]{0:T(1024)S(1)} %copy-done.42, bf16[768,2304]{1,0:T(8,128)(2,1)} %all-gather.10.cloned.1.call-done, ...), kind=kOutput, calls=%fused_computation.173 | convolution fusion | flops 7268201472 | bytes 35026944 | tf_op jit(solution)/shard_map/dot_general | solution.py:223
  587.4 5.8 fusion.127
  605.4 6.3 convolution_convert_fusion
  623.1 19.0 %fusion.99 = f32[768,2304]{1,0:T(8,128)} fusion(f32[2048,1152]{1,0:T(8,128)} %get-tuple-element.476, f32[2048,1152]{1,0:T(8,128)} %get-tuple-element.424, f32[2048,768]{0,1:T(8,128)} %copy-done.10, f32[768]{0:T(1024)S(1)} %copy-done.42, f32[2048]{0:T(1024)S(1)} %fusion.115, f32[2048]{0:T(1024)S(1)} %broadcast_multiply_fusion.2), kind=kOutput, calls=%fused_computation.189 | convolution fusion | flops 7263485952 | bytes 32263168 | tf_op jit(solution)/shard_map/dot_general | solution.py:222
  644.0 588.6 %while.31 = (s32[]{:T(128)}, f32[4,512,12,64]{1,0,3,2:T(4,128)}, f32[4,512,12,64]{1,0,3,2:T(4,128)}, bf16[4,512,12,64]{1,3,2,0:T(8,128)(2,1)}, bf16[4,512,12,64]...) while((s32[]{:T(128)}, f32[4,512,12,64]{1,0,3,2:T(4,128)}, ...), condition=%wide.region_12.13_spmd, body=%wide.region_10.12_spmd.sunk | while | flops 1587027968 | bytes 218263584 | solution.py:232
  668.3 7.0 fusion.194
  681.7 5.4 fusion.201
  707.4 6.7 multiply_reduce_fusion.5
  721.9 31.2 %dynamic_update_slice.45 = f32[4,512,12,64]{1,0,3,2:T(4,128)} dynamic-update-slice(f32[4,512,12,64]{1,0,3,2:T(4,128)} %get-tuple-element.751, f32[1,512,12,64]{1,0,3,2:T(1,128)} %bitcast.200, s32[]{:T(128)} %get-tuple-element.749, s32[]{:T(128)} %constant.218.clone.1..sunk.1, s32[]{:T(128)} %constant.218.clone.1..sunk.1, s32[]{:T(128)} %constant.218.clone.1..sunk.1) | dynamic-update-slice | bytes 3145732 | tf_op jit(solution)/shard_map/while/body/jit(dynamic_update_index_in_dim)/dynamic_update_slice | solution.py:232
  760.5 31.1 %dynamic_update_slice.44 = f32[4,512,12,64]{1,0,3,2:T(4,128)} dynamic-update-slice(f32[4,512,12,64]{1,0,3,2:T(4,128)} %get-tuple-element.750, f32[1,512,12,64]{1,0,3,2:T(1,128)} %bitcast.199, s32[]{:T(128)} %get-tuple-element.749, s32[]{:T(128)} %constant.218.clone.1..sunk.1, s32[]{:T(128)} %constant.218.clone.1..sunk.1, s32[]{:T(128)} %constant.218.clone.1..sunk.1) | dynamic-update-slice | bytes 3145732 | tf_op jit(solution)/shard_map/while/body/jit(dynamic_update_index_in_dim)/dynamic_update_slice | solution.py:232
  815.8 6.8 fusion.194
  829.1 5.3 fusion.201
  854.6 6.7 multiply_reduce_fusion.5
  869.2 31.0 %dynamic_update_slice.45 = f32[4,512,12,64]{1,0,3,2:T(4,128)} dynamic-update-slice(f32[4,512,12,64]{1,0,3,2:T(4,128)} %get-tuple-element.751, f32[1,512,12,64]{1,0,3,2:T(1,128)} %bitcast.200, s32[]{:T(128)} %get-tuple-element.749, s32[]{:T(128)} %constant.218.clone.1..sunk.1, s32[]{:T(128)} %constant.218.clone.1..sunk.1, s32[]{:T(128)} %constant.218.clone.1..sunk.1) | dynamic-update-slice | bytes 3145732 | tf_op jit(solution)/shard_map/while/body/jit(dynamic_update_index_in_dim)/dynamic_update_slice | solution.py:232
  907.5 31.0 %dynamic_update_slice.44 = f32[4,512,12,64]{1,0,3,2:T(4,128)} dynamic-update-slice(f32[4,512,12,64]{1,0,3,2:T(4,128)} %get-tuple-element.750, f32[1,512,12,64]{1,0,3,2:T(1,128)} %bitcast.199, s32[]{:T(128)} %get-tuple-element.749, s32[]{:T(128)} %constant.218.clone.1..sunk.1, s32[]{:T(128)} %constant.218.clone.1..sunk.1, s32[]{:T(128)} %constant.218.clone.1..sunk.1) | dynamic-update-slice | bytes 3145732 | tf_op jit(solution)/shard_map/while/body/jit(dynamic_update_index_in_dim)/dynamic_update_slice | solution.py:232
  962.7 6.8 fusion.194
  975.9 5.3 fusion.201
  1001.5 6.7 multiply_reduce_fusion.5
  1016.0 31.0 %dynamic_update_slice.45 = f32[4,512,12,64]{1,0,3,2:T(4,128)} dynamic-update-slice(f32[4,512,12,64]{1,0,3,2:T(4,128)} %get-tuple-element.751, f32[1,512,12,64]{1,0,3,2:T(1,128)} %bitcast.200, s32[]{:T(128)} %get-tuple-element.749, s32[]{:T(128)} %constant.218.clone.1..sunk.1, s32[]{:T(128)} %constant.218.clone.1..sunk.1, s32[]{:T(128)} %constant.218.clone.1..sunk.1) | dynamic-update-slice | bytes 3145732 | tf_op jit(solution)/shard_map/while/body/jit(dynamic_update_index_in_dim)/dynamic_update_slice | solution.py:232
  1054.4 31.0 %dynamic_update_slice.44 = f32[4,512,12,64]{1,0,3,2:T(4,128)} dynamic-update-slice(f32[4,512,12,64]{1,0,3,2:T(4,128)} %get-tuple-element.750, f32[1,512,12,64]{1,0,3,2:T(1,128)} %bitcast.199, s32[]{:T(128)} %get-tuple-element.749, s32[]{:T(128)} %constant.218.clone.1..sunk.1, s32[]{:T(128)} %constant.218.clone.1..sunk.1, s32[]{:T(128)} %constant.218.clone.1..sunk.1) | dynamic-update-slice | bytes 3145732 | tf_op jit(solution)/shard_map/while/body/jit(dynamic_update_index_in_dim)/dynamic_update_slice | solution.py:232
  1109.5 6.8 fusion.194
  1122.8 5.3 fusion.201
  1148.3 6.7 multiply_reduce_fusion.5
  1162.9 31.0 %dynamic_update_slice.45 = f32[4,512,12,64]{1,0,3,2:T(4,128)} dynamic-update-slice(f32[4,512,12,64]{1,0,3,2:T(4,128)} %get-tuple-element.751, f32[1,512,12,64]{1,0,3,2:T(1,128)} %bitcast.200, s32[]{:T(128)} %get-tuple-element.749, s32[]{:T(128)} %constant.218.clone.1..sunk.1, s32[]{:T(128)} %constant.218.clone.1..sunk.1, s32[]{:T(128)} %constant.218.clone.1..sunk.1) | dynamic-update-slice | bytes 3145732 | tf_op jit(solution)/shard_map/while/body/jit(dynamic_update_index_in_dim)/dynamic_update_slice | solution.py:232
  1201.2 31.0 %dynamic_update_slice.44 = f32[4,512,12,64]{1,0,3,2:T(4,128)} dynamic-update-slice(f32[4,512,12,64]{1,0,3,2:T(4,128)} %get-tuple-element.750, f32[1,512,12,64]{1,0,3,2:T(1,128)} %bitcast.199, s32[]{:T(128)} %get-tuple-element.749, s32[]{:T(128)} %constant.218.clone.1..sunk.1, s32[]{:T(128)} %constant.218.clone.1..sunk.1, s32[]{:T(128)} %constant.218.clone.1..sunk.1) | dynamic-update-slice | bytes 3145732 | tf_op jit(solution)/shard_map/while/body/jit(dynamic_update_index_in_dim)/dynamic_update_slice | solution.py:232
  1232.6 8.5 reshape.604
  1241.1 8.5 reshape.606
  1249.6 8.5 copy.168
  1258.1 8.6 copy.169
  1271.8 9.6 slice_negate_fusion
  1281.4 6.8 maximum_multiply_fusion.2
  1288.3 8.4 fusion.88
  1296.8 14.2 fusion.96
  1311.0 9.1 fusion.138
  1320.1 89.3 %fusion = f32[40,768]{1,0:T(8,128)S(1)} fusion(f32[1152,768]{1,0:T(8,128)} %fusion.138), kind=kCustom, calls=%all-reduce-scatter | all-reduce-scatter fusion | flops 983041 | bytes 3661824
  1415.2 11.3 fusion.86
  1433.7 38.5 %all-reduce.3 = f32[2,768]{1,0:T(2,128)S(1)} all-reduce(f32[2,768]{1,0:T(2,128)S(1)} %pad_maximum_fusion.5), channel_id=6, replica_groups=mesh['fsdp'=32] {'fsdp'}, use_global_device_ids=true, to_apply=%region_21.22.clone | all-reduce | flops 1536 | bytes 12288
  1472.3 10.8 add_convert_fusion.1
  1483.1 6.7 add_add_fusion.4
  1490.5 6.7 copy.147
  (580 shorter events, 607.7 us)
Async XLA Ops:
  7.2 63.2 %all-gather.12.cloned.1.call-start = ((), (), s32[]{:S(2)}) async-start(), calls=%async_computation.10 | async-start | bytes 2027520 | tf_op jit(solution)/shard_map/all_gather | solution.py:176
  8.8 123.9 %all-gather.6.cloned.1.call-start = ((), (), s32[]{:S(2)}) async-start(), calls=%async_computation.4 | async-start | bytes 3649536 | tf_op jit(solution)/shard_map/all_gather | solution.py:173
  10.5 499.1 %all-gather.8.cloned.1.call-start = ((), (), s32[]{:S(2)}) async-start(), calls=%async_computation.5 | async-start | bytes 1216512 | tf_op jit(solution)/shard_map/all_gather | solution.py:174
  13.3 23.2 %all-to-all-start = ((bf16[32,2,24]{2,1,0:T(2,128)(2,1)}), bf16[32,2,24]{2,1,0:T(2,128)(2,1)S(1)}, u32[]{:S(2)}, u32[]{:S(2)}) async-start(bf16[32,2,24]{2,1,0:T(2,128)(2,1)} %stack.4), calls=%async_computation | async-start | bytes 32768 | tf_op jit(solution)/shard_map/all_to_all | solution.py:178
  20.7 498.4 %all-gather.10.cloned.1.call-start = ((), (), s32[]{:S(2)}) async-start(), calls=%async_computation.6 | async-start | bytes 3649536 | tf_op jit(solution)/shard_map/all_gather | solution.py:175
  22.3 1482.7 %reduce-scatter.9.cloned.1.call-start = ((), (), s32[]{:S(2)}) async-start(), calls=%async_computation.8 | async-start | bytes 2433024 | tf_op jit(solution)/shard_map/reduce_scatter | solution.py:252
  22.4 9.3 copy-start.44
  25.6 107.1 %copy-start.5 = (bf16[2048,768]{0,1:T(8,128)(2,1)}, bf16[2048,768]{0,1:T(8,128)(2,1)S(1)}, u32[]{:S(2)}) copy-start(bf16[2048,768]{0,1:T(8,128)(2,1)S(1)} %copy.124) | copy-start | bytes 9437188
  26.1 106.6 %copy-start.30 = (f32[2048]{0:T(1024)}, f32[2048]{0:T(1024)S(1)}, u32[]{:S(2)}) copy-start(f32[2048]{0:T(1024)S(1)} %broadcast_multiply_fusion.3) | copy-start | bytes 24580
  27.0 9.5 copy-start.36
  27.0 119.4 %copy-start.32 = (f32[2048]{0:T(1024)}, f32[2048]{0:T(1024)S(1)}, u32[]{:S(2)}) copy-start(f32[2048]{0:T(1024)S(1)} %fusion.114) | copy-start | bytes 24580
  27.1 9.4 copy-start.38
  36.7 109.7 %copy-start.40 = (f32[768]{0:T(1024)}, f32[768]{0:T(1024)S(1)}, u32[]{:S(2)}) copy-start(f32[768]{0:T(1024)S(1)} %mul.471) | copy-start | bytes 9220
  280.0 7.0 copy-start.17
  342.5 7.0 copy-start.17
  405.0 7.0 copy-start.17
  467.5 7.0 copy-start.17
  501.4 8.2 copy-start.2
  501.4 8.2 copy-start.28
  519.0 11.4 copy-start.19
  519.1 11.3 copy-start.26
  598.0 7.4 copy-start.51
  602.1 904.7 %reduce-scatter.11.cloned.1.call-start = ((), (), s32[]{:S(2)}) async-start(), calls=%async_computation.9 | async-start | bytes 7299072 | tf_op jit(solution)/shard_map/reduce_scatter | solution.py:253
  642.1 866.7 %reduce-scatter.7.cloned.1.call-start = ((), (), s32[]{:S(2)}) async-start(), calls=%async_computation.7 | async-start | bytes 7299072 | tf_op jit(solution)/shard_map/reduce_scatter | solution.py:251
  658.4 16.9 %copy-start.13 = (bf16[1,128,12,64]{1,3,2,0:T(8,128)(2,1)}, bf16[1,128,12,64]{1,3,2,0:T(8,128)(2,1)S(1)}, u32[]{:S(2)}) copy-start(bf16[1,128,12,64]{1,3,2,0:T(8,128)(2,1)S(1)} %get-tuple-element.675) | copy-start | bytes 589828 | tf_op jit(solution)/shard_map/while
  705.9 8.3 slice-start
  707.3 6.8 slice-start.1
  707.3 6.8 slice-start.2
  707.3 6.8 copy-start.16
  719.3 33.9 %copy-start.14 = (bf16[1,128,12,64]{1,3,2,0:T(8,128)(2,1)S(1)}, bf16[1,128,12,64]{1,3,2,0:T(8,128)(2,1)}, u32[]{:S(2)}) copy-start(bf16[1,128,12,64]{1,3,2,0:T(8,128)(2,1)} %copy-done.13) | copy-start | bytes 589828 | tf_op jit(solution)/shard_map/while
  805.8 16.8 %copy-start.13 = (bf16[1,128,12,64]{1,3,2,0:T(8,128)(2,1)}, bf16[1,128,12,64]{1,3,2,0:T(8,128)(2,1)S(1)}, u32[]{:S(2)}) copy-start(bf16[1,128,12,64]{1,3,2,0:T(8,128)(2,1)S(1)} %get-tuple-element.675) | copy-start | bytes 589828 | tf_op jit(solution)/shard_map/while
  853.1 8.3 slice-start
  854.6 6.8 slice-start.1
  854.6 6.8 slice-start.2
  854.6 6.8 copy-start.16
  866.5 33.7 %copy-start.14 = (bf16[1,128,12,64]{1,3,2,0:T(8,128)(2,1)S(1)}, bf16[1,128,12,64]{1,3,2,0:T(8,128)(2,1)}, u32[]{:S(2)}) copy-start(bf16[1,128,12,64]{1,3,2,0:T(8,128)(2,1)} %copy-done.13) | copy-start | bytes 589828 | tf_op jit(solution)/shard_map/while
  952.8 16.7 %copy-start.13 = (bf16[1,128,12,64]{1,3,2,0:T(8,128)(2,1)}, bf16[1,128,12,64]{1,3,2,0:T(8,128)(2,1)S(1)}, u32[]{:S(2)}) copy-start(bf16[1,128,12,64]{1,3,2,0:T(8,128)(2,1)S(1)} %get-tuple-element.675) | copy-start | bytes 589828 | tf_op jit(solution)/shard_map/while
  999.9 8.3 slice-start
  1001.4 6.8 slice-start.1
  1001.4 6.8 slice-start.2
  1013.4 33.7 %copy-start.14 = (bf16[1,128,12,64]{1,3,2,0:T(8,128)(2,1)S(1)}, bf16[1,128,12,64]{1,3,2,0:T(8,128)(2,1)}, u32[]{:S(2)}) copy-start(bf16[1,128,12,64]{1,3,2,0:T(8,128)(2,1)} %copy-done.13) | copy-start | bytes 589828 | tf_op jit(solution)/shard_map/while
  1099.6 16.7 %copy-start.13 = (bf16[1,128,12,64]{1,3,2,0:T(8,128)(2,1)}, bf16[1,128,12,64]{1,3,2,0:T(8,128)(2,1)S(1)}, u32[]{:S(2)}) copy-start(bf16[1,128,12,64]{1,3,2,0:T(8,128)(2,1)S(1)} %get-tuple-element.675) | copy-start | bytes 589828 | tf_op jit(solution)/shard_map/while
  1146.8 8.3 slice-start
  1148.2 6.8 slice-start.1
  1148.3 6.8 slice-start.2
  1160.2 33.7 %copy-start.14 = (bf16[1,128,12,64]{1,3,2,0:T(8,128)(2,1)S(1)}, bf16[1,128,12,64]{1,3,2,0:T(8,128)(2,1)}, u32[]{:S(2)}) copy-start(bf16[1,128,12,64]{1,3,2,0:T(8,128)(2,1)} %copy-done.13) | copy-start | bytes 589828 | tf_op jit(solution)/shard_map/while
  1258.1 8.6 copy-start.20
  1271.8 9.6 copy-start.25
  1271.8 16.5 %slice-start.3 = ((s8[6291456]{0:T(1024)(128)(4,1)}), s8[2097152]{0:T(1024)(128)(4,1)S(1)}, s32[]{:S(2)}) async-start(s8[6291456]{0:T(1024)(128)(4,1)} %bitcast.205), calls=%async_computation.14 | async-start | bytes 4194304
  1281.4 6.9 slice-start.4
  1281.4 6.9 copy-start.24
  1288.3 8.5 copy-start.6
  1288.3 8.5 copy-start.31
  1288.3 8.4 copy-start.33
  1288.3 8.4 copy-start.41
  1409.4 90.6 %collective-permute-start = (f32[40,768]{1,0:T(8,128)S(1)}, f32[40,768]{1,0:T(8,128)}, u32[]{:S(2)}, u32[]{:S(2)}) collective-permute-start(f32[40,768]{1,0:T(8,128)S(1)} %fusion), channel_id=1, source_target_pairs={{0,1},{1,2},{2,3},{3,4},{4,5},{5,6},{6,7},{7,8},{8,9},{9,10},{10,1... | collective-permute-start | bytes 368648
  1411.4 88.6 %collective-permute-start.1 = (f32[40,768]{1,0:T(8,128)S(1)}, f32[40,768]{1,0:T(8,128)}, u32[]{:S(2)}, u32[]{:S(2)}) collective-permute-start(f32[40,768]{1,0:T(8,128)S(1)} %fusion), channel_id=1, source_target_pairs={{0,2},{1,3},{2,4},{3,5},{4,6},{5,7},{6,8},{7,9},{8,10},{9,11},{10,... | collective-permute-start | bytes 368648
  1413.3 86.7 %collective-permute-start.2 = (f32[40,768]{1,0:T(8,128)S(1)}, f32[40,768]{1,0:T(8,128)}, u32[]{:S(2)}, u32[]{:S(2)}) collective-permute-start(f32[40,768]{1,0:T(8,128)S(1)} %fusion), channel_id=1, source_target_pairs={{0,3},{1,4},{2,5},{3,6},{4,7},{5,8},{6,9},{7,10},{8,11},{9,12},{10... | collective-permute-start | bytes 368648
  1415.2 11.3 copy-start.37
  1432.4 67.6 %collective-permute-start.3 = (f32[4,768]{1,0:T(4,128)S(1)}, f32[4,768]{1,0:T(4,128)S(1)}, u32[]{:S(2)}, u32[]{:S(2)}) collective-permute-start(f32[4,768]{1,0:T(4,128)S(1)} %slice.364), channel_id=1, source_target_pairs={{0,4},{1,5},{2,6},{3,7},{4,8},{5,9},{6,10},{7,11},{8,12},{9,13},{1... | collective-permute-start | bytes 36872
  1472.3 10.8 copy-start.9
  1472.3 10.8 copy-start.12
  1472.3 10.8 copy-start.35
  1497.2 9.5 copy-start.27
  (41 other events, 154.0 us)
Sparse Core Ops, SparseCore 0:
  11.5 58.8 all-gather.11
  73.8 58.8 all-gather.5
  136.2 52.8 all-gather.7
  192.4 58.9 all-gather.9
  602.2 97.9 reduce-scatter.8
  707.2 118.1 reduce-scatter.10
  1311.2 133.5 reduce-scatter.6
